TPU v7x, 32 devices: a whole 2x2x4 slice. The times are simulated.
32 devices in a mesh: groups: 2 (over y), feat: 8 (over z, core), tok: 2 (over x).
Axes of the slice: x: 2, y: 2, z: 4, core: 2. Of those that a mesh axis runs over, the one named last changes fastest.
Arguments:
- tokens: bfloat16 [1024, 4096], P(('groups', 'feat'), 'tok'), parts along dimension 0, may hold values from -6 to 6
- out_grad: bfloat16 [1024, 4096], P(('groups', 'feat'), 'tok'), parts along dimension 0, may hold values from -0.75 to 0.75
- gate_weight: bfloat16 [4096, 14336], P('tok', 'feat'), may hold values from -0.09375 to 0.09375
- up_weight: bfloat16 [4096, 14336], P('tok', 'feat'), may hold values from -0.09375 to 0.09375
- down_weight: bfloat16 [14336, 4096], P('feat', 'tok'), may hold values from -0.046875 to 0.046875
Outputs:
- grad_gate: bfloat16 [8192, 14336], P(('groups', 'tok'), 'feat'), parts along dimension 0
- grad_up: bfloat16 [8192, 14336], P(('groups', 'tok'), 'feat'), parts along dimension 0
- grad_down: bfloat16 [28672, 4096], P(('groups', 'feat'), 'tok'), parts along dimension 0
There are 2 independent parts, one for each index of `groups`. A program takes and returns all parts, laid end to end along the dimension named above; an argument that names none is the same for every part. Nothing has to cross between parts.
All inputs are finite; a program needn't handle non-finite values.
Results may differ from a plain program's by a relative error of at most 0.005.
Values may be sent and summed in bfloat16 or wider, within the bound.
A program may use at most 128 MiB of HBM per device.

v0:
```python
import jax
import jax.numpy as jnp
from jax import lax
from jax.sharding import PartitionSpec as P


def contract_rows(left, right):
    return lax.dot_general(
        left, right, (((0,), (0,)), ((), ())), preferred_element_type=jnp.float32
    )


def swiglu_parts(gate, up, grad_hidden):
    sigmoid_gate = jax.nn.sigmoid(gate)
    activated = gate * sigmoid_gate
    hidden = (activated * up).astype(jnp.bfloat16)
    gate_delta = (grad_hidden * up * sigmoid_gate * (1.0 + gate * (1.0 - sigmoid_gate))).astype(
        jnp.bfloat16
    )
    up_delta = (grad_hidden * activated).astype(jnp.bfloat16)
    return (hidden, gate_delta, up_delta)


def shards(tokens, out_grad, gate_weight, up_weight, down_weight):
    token_rows, grad_rows = (
        lax.all_gather(tokens, "feat", axis=0, tiled=True),
        lax.all_gather(out_grad, "feat", axis=0, tiled=True),
    )
    gate_part = jnp.dot(token_rows, gate_weight, preferred_element_type=jnp.float32)
    up_part = jnp.dot(token_rows, up_weight, preferred_element_type=jnp.float32)
    hidden_part = lax.dot_general(
        grad_rows, down_weight, (((1,), (1,)), ((), ())), preferred_element_type=jnp.float32
    )
    gate, up = (
        lax.psum_scatter(gate_part, "tok", scatter_dimension=0, tiled=True),
        lax.psum_scatter(up_part, "tok", scatter_dimension=0, tiled=True),
    )
    grad_hidden = lax.psum_scatter(hidden_part, "tok", scatter_dimension=0, tiled=True)
    hidden, gate_delta, up_delta = swiglu_parts(gate, up, grad_hidden)
    hidden, gate_delta, up_delta = (
        lax.all_gather(hidden, "tok", axis=0, tiled=True),
        lax.all_gather(gate_delta, "tok", axis=0, tiled=True),
        lax.all_gather(up_delta, "tok", axis=0, tiled=True),
    )
    grad_gate = contract_rows(token_rows, gate_delta).astype(jnp.bfloat16)
    grad_up = contract_rows(token_rows, up_delta).astype(jnp.bfloat16)
    grad_down = contract_rows(hidden, grad_rows).astype(jnp.bfloat16)
    return (grad_gate, grad_up, grad_down)


def solution(mesh):
    return jax.shard_map(
        shards,
        mesh=mesh,
        in_specs=(
            P(("groups", "feat"), "tok"),
            P(("groups", "feat"), "tok"),
            P("tok", "feat"),
            P("tok", "feat"),
            P("feat", "tok"),
        ),
        out_specs=(
            P(("groups", "tok"), "feat"),
            P(("groups", "tok"), "feat"),
            P(("groups", "feat"), "tok"),
        ),
        check_vma=False,
    )
```

profile of v0, /device:TPU:0, one launch (start us, length us, event | category | flops | bytes accessed | tf_op | source)
XLA Modules:
  0.0 340.8 jit_solution(12979034745607124488)
XLA Ops:
  7.2 0.0 all-gather.8.cloned.1.call-start
  7.2 0.7 all-gather.8.cloned.1.call-update
  7.9 0.0 all-gather.6.cloned.1.call-start
  7.9 0.7 all-gather.6.cloned.1.call-update
  8.6 0.0 reduce-scatter.6.cloned.1.call-start
  8.7 32.7 %all-gather.8.cloned.1.call-done = bf16[512,2048]{1,0:T(8,128)(2,1)} async-done(((bf16[64,2048]{1,0:T(8,128)(2,1)}), bf16[512,2048]{1,0:T(8,128)(2,1)}) %all-gather.8.cloned.1.call-update) | async-done | bytes 2097168 | tf_op jit(solution)/shard_map/all_gather | solution.py:26
  41.4 9.5 %fusion.4 = f32[512,1792]{1,0:T(8,128)} fusion(bf16[512,2048]{1,0:T(8,128)(2,1)} %all-gather.8.cloned.1.call-done, bf16[2048,1792]{1,0:T(8,128)(2,1)} %param.8), kind=kOutput, calls=%fused_computation.11 | convolution fusion | flops 3758096384 | bytes 13107200 | tf_op jit(solution)/shard_map/dot_general | solution.py:30
  50.9 0.0 copy-start.1
  50.9 0.0 reduce-scatter.6.cloned.1.call-update
  51.0 0.0 reduce-scatter.8.cloned.1.call-start
  51.0 1.5 copy-done.1
  52.5 8.9 %fusion.5 = f32[512,1792]{1,0:T(8,128)} fusion(bf16[512,2048]{1,0:T(8,128)(2,1)S(1)} %copy-done.1, bf16[2048,1792]{1,0:T(8,128)(2,1)} %param.7), kind=kOutput, calls=%fused_computation.12 | convolution fusion | flops 3758096384 | bytes 13107200 | tf_op jit(solution)/shard_map/dot_general | solution.py:29
  61.4 0.0 reduce-scatter.8.cloned.1.call-update
  61.4 0.0 reduce-scatter.4.cloned.1.call-start
  61.5 10.2 %all-gather.6.cloned.1.call-done = bf16[512,2048]{1,0:T(8,128)(2,1)} async-done(((bf16[64,2048]{1,0:T(8,128)(2,1)}), bf16[512,2048]{1,0:T(8,128)(2,1)}) %all-gather.6.cloned.1.call-update) | async-done | bytes 2097168 | tf_op jit(solution)/shard_map/all_gather | solution.py:27
  71.7 9.9 %fusion.3 = f32[512,1792]{1,0:T(8,128)} fusion(bf16[512,2048]{1,0:T(8,128)(2,1)} %all-gather.6.cloned.1.call-done, bf16[1792,2048]{1,0:T(8,128)(2,1)} %param.9), kind=kOutput, calls=%fused_computation.10 | convolution fusion | flops 3758096384 | bytes 13107200 | tf_op jit(solution)/shard_map/dot_general | solution.py:31
  81.5 0.0 reduce-scatter.4.cloned.1.call-update
  81.6 0.0 all-gather.12.cloned.1.call-start
  81.6 41.5 %reduce-scatter.6.cloned.1.call-done = f32[256,1792]{1,0:T(8,128)} async-done(((f32[512,1792]{1,0:T(8,128)}), f32[256,1792]{1,0:T(8,128)}) %reduce-scatter.6.cloned.1.call-update) | async-done | bytes 1835024 | tf_op jit(solution)/shard_map/reduce_scatter | solution.py:36
  123.1 51.9 %reduce-scatter.8.cloned.1.call-done = f32[256,1792]{1,0:T(8,128)} async-done(((f32[512,1792]{1,0:T(8,128)}), f32[256,1792]{1,0:T(8,128)}) %reduce-scatter.8.cloned.1.call-update) | async-done | bytes 1835024 | tf_op jit(solution)/shard_map/reduce_scatter | solution.py:35
  175.0 51.8 %reduce-scatter.4.cloned.1.call-done = f32[256,1792]{1,0:T(8,128)} async-done(((f32[512,1792]{1,0:T(8,128)}), f32[256,1792]{1,0:T(8,128)}) %reduce-scatter.4.cloned.1.call-update) | async-done | bytes 1835024 | tf_op jit(solution)/shard_map/reduce_scatter | solution.py:38
  226.8 5.0 %multiply_convert_fusion = (bf16[256,1792]{1,0:T(8,128)(2,1)}, bf16[256,1792]{1,0:T(8,128)(2,1)}, bf16[256,1792]{1,0:T(8,128)(2,1)}) fusion(f32[256,1792]{1,0:T(8,128)} %reduce-scatter.6.cloned.1.call-done, f32[256,1792]{1,0:T(8,128)} %reduce-scatter.8.cloned.1.call-done, f32[256,1792]{1,0:T(8,128)} %reduce-scatter.4.cloned.1.call-done), kind=kLoop, calls=%fused_computation.5 | loop fusion | flops 6881280 | bytes 8257536 | tf_op jit(solution)/shard_map/convert_element_type | solution.py:16
  231.9 0.0 all-gather.12.cloned.1.call-update
  231.9 0.0 all-gather.10.cloned.1.call-start
  231.9 0.7 all-gather.10.cloned.1.call-update
  232.6 0.2 all-gather.14.cloned.1.call-start
  232.9 0.5 all-gather.14.cloned.1.call-update
  233.4 28.8 %all-gather.12.cloned.1.call-done = bf16[512,1792]{1,0:T(8,128)(2,1)} async-done(((bf16[256,1792]{1,0:T(8,128)(2,1)}), bf16[512,1792]{1,0:T(8,128)(2,1)}) %all-gather.12.cloned.1.call-update) | async-done | bytes 1835024 | tf_op jit(solution)/shard_map/all_gather | solution.py:43
  262.2 7.5 %fusion.1 = bf16[2048,1792]{0,1:T(8,128)(2,1)} fusion(bf16[512,1792]{1,0:T(8,128)(2,1)} %all-gather.12.cloned.1.call-done, bf16[512,2048]{1,0:T(8,128)(2,1)S(1)} %copy-done.1), kind=kOutput, calls=%fused_computation.4 | convolution fusion | flops 3761766400 | bytes 11272192 | tf_op jit(solution)/shard_map/dot_general | solution.py:8
  269.8 10.0 %copy.9 = bf16[2048,1792]{1,0:T(8,128)(2,1)} copy(bf16[2048,1792]{0,1:T(8,128)(2,1)} %fusion.1) | data formatting | bytes 14680064
  279.8 14.8 %all-gather.10.cloned.1.call-done = bf16[512,1792]{1,0:T(8,128)(2,1)} async-done(((bf16[256,1792]{1,0:T(8,128)(2,1)}), bf16[512,1792]{1,0:T(8,128)(2,1)}) %all-gather.10.cloned.1.call-update) | async-done | bytes 1835024 | tf_op jit(solution)/shard_map/all_gather | solution.py:42
  294.6 7.6 %fusion = bf16[2048,1792]{0,1:T(8,128)(2,1)} fusion(bf16[512,1792]{1,0:T(8,128)(2,1)} %all-gather.10.cloned.1.call-done, bf16[512,2048]{1,0:T(8,128)(2,1)S(1)} %copy-done.1), kind=kOutput, calls=%fused_computation.3 | convolution fusion | flops 3761766400 | bytes 11272192 | tf_op jit(solution)/shard_map/dot_general | solution.py:8
  302.2 0.0 copy-start
  302.2 10.2 %copy.8 = bf16[2048,1792]{1,0:T(8,128)(2,1)} copy(bf16[2048,1792]{0,1:T(8,128)(2,1)} %fusion) | data formatting | bytes 14680064
  312.3 14.1 %all-gather.14.cloned.1.call-done = bf16[512,1792]{1,0:T(8,128)(2,1)} async-done(((bf16[256,1792]{1,0:T(8,128)(2,1)}), bf16[512,1792]{1,0:T(8,128)(2,1)}) %all-gather.14.cloned.1.call-update) | async-done | bytes 1835024 | tf_op jit(solution)/shard_map/all_gather | solution.py:41
  326.4 0.0 copy-done
  326.4 7.6 %convolution_convert_fusion = bf16[1792,2048]{1,0:T(8,128)(2,1)} fusion(bf16[512,1792]{1,0:T(8,128)(2,1)} %all-gather.14.cloned.1.call-done, bf16[512,2048]{1,0:T(8,128)(2,1)S(1)} %copy-done), kind=kOutput, calls=%fused_computation | convolution fusion | flops 3761766400 | bytes 11272192 | tf_op jit(solution)/shard_map/dot_general | solution.py:8
Async XLA Ops:
  7.2 34.3 %all-gather.8.cloned.1.call-start = ((), (), s32[]{:S(2)}) async-start(), calls=%async_computation.5 | async-start | bytes 2359296 | tf_op jit(solution)/shard_map/all_gather | solution.py:26
  7.9 63.8 %all-gather.6.cloned.1.call-start = ((), (), s32[]{:S(2)}) async-start(), calls=%async_computation.3 | async-start | bytes 2359296 | tf_op jit(solution)/shard_map/all_gather | solution.py:27
  8.6 114.5 %reduce-scatter.6.cloned.1.call-start = ((), (), s32[]{:S(2)}) async-start(), calls=%async_computation.6 | async-start | bytes 5505024 | tf_op jit(solution)/shard_map/reduce_scatter | solution.py:36
  50.9 1.6 copy-start.1
  51.0 124.1 %reduce-scatter.8.cloned.1.call-start = ((), (), s32[]{:S(2)}) async-start(), calls=%async_computation.7 | async-start | bytes 5505024 | tf_op jit(solution)/shard_map/reduce_scatter | solution.py:35
  61.4 165.4 %reduce-scatter.4.cloned.1.call-start = ((), (), s32[]{:S(2)}) async-start(), calls=%async_computation.4 | async-start | bytes 5505024 | tf_op jit(solution)/shard_map/reduce_scatter | solution.py:38
  81.6 180.6 %all-gather.12.cloned.1.call-start = ((), (), s32[]{:S(2)}) async-start(), calls=%async_computation.9 | async-start | bytes 2752512 | tf_op jit(solution)/shard_map/all_gather | solution.py:43
  231.9 62.7 %all-gather.10.cloned.1.call-start = ((), (), s32[]{:S(2)}) async-start(), calls=%async_computation.8 | async-start | bytes 2752512 | tf_op jit(solution)/shard_map/all_gather | solution.py:42
  232.6 93.8 %all-gather.14.cloned.1.call-start = ((), (), s32[]{:S(2)}) async-start(), calls=%async_computation.10 | async-start | bytes 2752512 | tf_op jit(solution)/shard_map/all_gather | solution.py:41
  302.2 24.3 %copy-start = (bf16[512,2048]{1,0:T(8,128)(2,1)S(1)}, bf16[512,2048]{1,0:T(8,128)(2,1)}, u32[]{:S(2)}) copy-start(bf16[512,2048]{1,0:T(8,128)(2,1)} %all-gather.6.cloned.1.call-done) | copy-start | bytes 6291460
Sparse Core Ops, SparseCore 0:
  9.6 31.7 all-gather.7
  43.0 28.5 all-gather.5
  74.5 48.5 reduce-scatter.5
  125.9 49.0 reduce-scatter.7
  177.7 49.0 reduce-scatter.3
  232.0 30.1 all-gather.11
  264.4 30.1 all-gather.9
  296.2 30.1 all-gather.13
where the time goes:
time: 342 us; the launch traced here: 341 us
  waiting for transfers between devices  248 us (73%)
  matrix products  50.9 us (15%)
  local copies, waits for them, and re-layouts  21.7 us (6%)
  between operations  14.1 us (4%)
  other arithmetic  5.03 us (1%)
    reduce_scatter x1, waiting for transfers between devices, shards(): lax.psum_scatter(gate_part, 'tok', scatter_dimension=0, tiled=True)  51.9 us
    reduce_scatter x1, waiting for transfers between devices, shards(): lax.psum_scatter(hidden_part, 'tok', scatter_dimension=0, tiled=True)  51.8 us
    reduce_scatter x1, waiting for transfers between devices, shards(): lax.psum_scatter(up_part, 'tok', scatter_dimension=0, tiled=True)  41.5 us
    all_gather x1, waiting for transfers between devices, shards(): lax.all_gather(tokens, 'feat', axis=0, tiled=True)  32.7 us
    all_gather x1, waiting for transfers between devices, shards(): lax.all_gather(up_delta, 'tok', axis=0, tiled=True)  28.8 us
    dot_general x3, matrix products, contract_rows(): lax.dot_general(left, right, (((0,), (0,)), ((), ())), preferred_element_...  22.7 us
    unnamed x6, local copies, waits for them, and re-layouts  21.7 us
    all_gather x1, waiting for transfers between devices, shards(): lax.all_gather(gate_delta, 'tok', axis=0, tiled=True)  14.8 us
  transfers between devices with their start and end apart: 8, of which 8 were waited for; matrix products, arithmetic and copies ran while one was open for 19% of the time, Pallas kernels for 0%

commit v1 on v0

--- a/solution.py
+++ b/solution.py
@@ -2,6 +2,28 @@
 import jax.numpy as jnp
 from jax import lax
 from jax.sharding import PartitionSpec as P
+
+
+def laid_out(blocks, dim):
+    blocks = jnp.moveaxis(blocks, 0, dim)
+    dims = blocks.shape
+    return blocks.reshape(*dims[:dim], dims[dim] * dims[dim + 1], *dims[dim + 2 :])
+
+
+def collect(x, axis, dim):
+    size = lax.axis_size(axis)
+    pairs = [(i, (i + 1) % size) for i in range(size)]
+    back = [(b, a) for a, b in pairs]
+    lower, upper = ([], [])
+    for turn in range(size - 1):
+        if turn % 2 == 0:
+            lower.append(lax.ppermute(lower[-1] if lower else x, axis, pairs))
+        else:
+            upper.append(lax.ppermute(upper[-1] if upper else x, axis, back))
+    pieces = jnp.stack([*lower[::-1], x, *upper])
+    shift = lax.axis_index(axis) - len(lower)
+    pieces = pieces[(jnp.arange(size) - shift) % size]
+    return laid_out(pieces, dim)
 
 
 def contract_rows(left, right):
@@ -24,7 +46,7 @@
 def shards(tokens, out_grad, gate_weight, up_weight, down_weight):
     token_rows, grad_rows = (
         lax.all_gather(tokens, "feat", axis=0, tiled=True),
-        lax.all_gather(out_grad, "feat", axis=0, tiled=True),
+        collect(out_grad, "feat", 0),
     )
     gate_part = jnp.dot(token_rows, gate_weight, preferred_element_type=jnp.float32)
     up_part = jnp.dot(token_rows, up_weight, preferred_element_type=jnp.float32)

time: 342 us -> 325 us (0.950)
  waiting for transfers between devices: 248 us -> 215 us
  starting transfers between devices: 0.5 us -> 11.7 us
  local copies, waits for them, and re-layouts: 21.7 us -> 25.9 us
    reduce_scatter x1, waiting for transfers between devices: 51.8 us -> 19 us  [shards(): lax.psum_scatter(hidden_part, 'tok', scatter_dimension=0, tiled=True)]
    ppermute x0 -> x7, waiting for transfers between devices: none -> 25.5 us  [the longest x4 25.5 us: collect(): lower.append(lax.ppermute(lower[-1] if lower else x, axis, pairs))]
    all_gather x1, waiting for transfers between devices: 32.7 us -> 8.57 us  [shards(): lax.all_gather(tokens, 'feat', axis=0, tiled=True)]
    all_gather x1, waiting for transfers between devices: 28.8 us -> 14.7 us  [shards(): lax.all_gather(up_delta, 'tok', axis=0, tiled=True)]
    all_gather x1, waiting for transfers between devices: 14.8 us -> 28.6 us  [shards(): lax.all_gather(gate_delta, 'tok', axis=0, tiled=True)]
    ppermute x0 -> x7, starting transfers between devices: none -> 11.2 us  [the longest x3 10.7 us: collect(): upper.append(lax.ppermute(upper[-1] if upper else x, axis, back))]
    reduce_scatter x1, waiting for transfers between devices: 41.5 us -> 51.8 us  [shards(): lax.psum_scatter(up_part, 'tok', scatter_dimension=0, tiled=True)]
    all_gather x1 -> x0, waiting for transfers between devices: 10.2 us -> none  [shards(): lax.all_gather(out_grad, 'feat', axis=0, tiled=True)]
  transfers between devices with their start and end apart: 8 -> 14, of which waited for: 8 -> 11; matrix products, arithmetic and copies ran while one was open for 19% -> 21% of each run, Pallas kernels for 0% -> 0%
where the time goes in v1:
time: 325 us; the launch traced here: 324 us
  waiting for transfers between devices  215 us (66%)
  matrix products  50.6 us (16%)
  local copies, waits for them, and re-layouts  25.9 us (8%)
  between operations  15.7 us (5%)
  starting transfers between devices  11.7 us (4%)
  other arithmetic  5.05 us (2%)
    reduce_scatter x1, waiting for transfers between devices, shards(): lax.psum_scatter(up_part, 'tok', scatter_dimension=0, tiled=True)  51.8 us
    reduce_scatter x1, waiting for transfers between devices, shards(): lax.psum_scatter(gate_part, 'tok', scatter_dimension=0, tiled=True)  51.7 us
    all_gather x1, waiting for transfers between devices, shards(): lax.all_gather(gate_delta, 'tok', axis=0, tiled=True)  28.6 us
    ppermute x4, waiting for transfers between devices, collect(): lower.append(lax.ppermute(lower[-1] if lower else x, axis, pairs))  25.5 us
    unnamed x17, local copies, waits for them, and re-layouts  23.9 us
    dot_general x3, matrix products, contract_rows(): lax.dot_general(left, right, (((0,), (0,)), ((), ())), preferred_element_...  22.7 us
    reduce_scatter x1, waiting for transfers between devices, shards(): lax.psum_scatter(hidden_part, 'tok', scatter_dimension=0, tiled=True)  19 us
    all_gather x1, waiting for transfers between devices, shards(): lax.all_gather(up_delta, 'tok', axis=0, tiled=True)  14.7 us
  transfers between devices with their start and end apart: 14, of which 11 were waited for; matrix products, arithmetic and copies ran while one was open for 21% of the time, Pallas kernels for 0%

profile of v1, /device:TPU:0, one launch (start us, length us, event | category | flops | bytes accessed | tf_op | source)
XLA Modules:
  0.0 324.2 jit_solution(15252756857739211305)
XLA Ops:
  8.0 0.0 copy-start.1
  8.0 0.0 all-gather.5.cloned.1.call-start
  8.1 0.5 collective-permute-start
  8.6 8.3 %collective-permute-done = bf16[64,2048]{1,0:T(8,128)(2,1)S(1)} collective-permute-done((bf16[64,2048]{1,0:T(8,128)(2,1)}, bf16[64,2048]{1,0:T(8,128)(2,1)S(1)}, u32[]{:S(2)}, u32[]{:S(2)}) %collective-permute-start) | collective-permute-done | bytes 262176 | tf_op jit(solution)/shard_map/ppermute | solution.py:20
  16.9 0.0 collective-permute-start.1
  16.9 3.5 %collective-permute-start.4 = (bf16[64,2048]{1,0:T(8,128)(2,1)}, bf16[64,2048]{1,0:T(8,128)(2,1)S(1)}, u32[]{:S(2)}, u32[]{:S(2)}) collective-permute-start(bf16[64,2048]{1,0:T(8,128)(2,1)} %param.6), channel_id=1, source_target_pairs={{2,0},{4,2},{6,4},{8,6},{10,8},{12,10},{14,12},{0,14},{3,1},{5,3},... | collective-permute-start | bytes 786440 | tf_op jit(solution)/shard_map/ppermute | solution.py:22
  20.4 5.9 %collective-permute-done.1 = bf16[64,2048]{1,0:T(8,128)(2,1)S(1)} collective-permute-done((bf16[64,2048]{1,0:T(8,128)(2,1)S(1)}, bf16[64,2048]{1,0:T(8,128)(2,1)S(1)}, u32[]{:S(2)}, u32[]{:S(2)}) %collective-permute-start.1) | collective-permute-done | bytes 262176 | tf_op jit(solution)/shard_map/ppermute | solution.py:20
  26.3 0.0 collective-permute-start.2
  26.3 0.0 collective-permute-done.4
  26.4 3.5 %collective-permute-start.5 = (bf16[64,2048]{1,0:T(8,128)(2,1)S(1)}, bf16[64,2048]{1,0:T(8,128)(2,1)S(1)}, u32[]{:S(2)}, u32[]{:S(2)}) collective-permute-start(bf16[64,2048]{1,0:T(8,128)(2,1)S(1)} %collective-permute-done.4), channel_id=1, source_target_pairs={{2,0},{4,2},{6,4},{8,6},{10,8},{12,10},{14,12},{0,14},{3,1},{5,3},... | collective-permute-start | bytes 786440 | tf_op jit(solution)/shard_map/ppermute | solution.py:22
  29.9 6.3 %collective-permute-done.2 = bf16[64,2048]{1,0:T(8,128)(2,1)S(1)} collective-permute-done((bf16[64,2048]{1,0:T(8,128)(2,1)S(1)}, bf16[64,2048]{1,0:T(8,128)(2,1)S(1)}, u32[]{:S(2)}, u32[]{:S(2)}) %collective-permute-start.2) | collective-permute-done | bytes 262176 | tf_op jit(solution)/shard_map/ppermute | solution.py:20
  36.2 0.0 copy-start.2
  36.2 0.0 collective-permute-start.3
  36.2 0.0 all-gather.5.cloned.1.call-update
  36.2 0.0 reduce-scatter.4.cloned.1.call-start
  36.3 0.0 collective-permute-done.5
  36.3 3.6 %collective-permute-start.6 = (bf16[64,2048]{1,0:T(8,128)(2,1)S(1)}, bf16[64,2048]{1,0:T(8,128)(2,1)S(1)}, u32[]{:S(2)}, u32[]{:S(2)}) collective-permute-start(bf16[64,2048]{1,0:T(8,128)(2,1)S(1)} %collective-permute-done.5), channel_id=1, source_target_pairs={{2,0},{4,2},{6,4},{8,6},{10,8},{12,10},{14,12},{0,14},{3,1},{5,3},... | collective-permute-start | bytes 786440 | tf_op jit(solution)/shard_map/ppermute | solution.py:22
  39.9 0.0 copy-done.2
  39.9 4.9 %collective-permute-done.3 = bf16[64,2048]{1,0:T(8,128)(2,1)} collective-permute-done((bf16[64,2048]{1,0:T(8,128)(2,1)S(1)}, bf16[64,2048]{1,0:T(8,128)(2,1)}, u32[]{:S(2)}, u32[]{:S(2)}) %collective-permute-start.3) | collective-permute-done | bytes 262176 | tf_op jit(solution)/shard_map/ppermute | solution.py:20
  44.8 1.0 bitcast_dynamic-update-slice_fusion.7
  45.8 1.0 bitcast_dynamic-update-slice_fusion.6
  46.9 0.0 copy-done.1
  47.0 0.0 collective-permute-done.6
  47.0 2.0 gather_fusion
  49.0 9.6 %fusion.5 = f32[512,1792]{1,0:T(8,128)} fusion(bf16[512,2048]{1,0:T(8,128)(2,1)} %bitcast.35, bf16[1792,2048]{1,0:T(8,128)(2,1)} %param.9), kind=kOutput, calls=%fused_computation.26 | convolution fusion | flops 3758096384 | bytes 13107200 | tf_op jit(solution)/shard_map/dot_general | solution.py:53
  58.6 0.0 reduce-scatter.4.cloned.1.call-update
  58.7 0.0 reduce-scatter.6.cloned.1.call-start
  58.7 8.6 %all-gather.5.cloned.1.call-done = bf16[512,2048]{1,0:T(8,128)(2,1)} async-done(((bf16[64,2048]{1,0:T(8,128)(2,1)}), bf16[512,2048]{1,0:T(8,128)(2,1)}) %all-gather.5.cloned.1.call-update) | async-done | bytes 2097168 | tf_op jit(solution)/shard_map/all_gather | solution.py:48
  67.3 9.5 %fusion.6 = f32[512,1792]{1,0:T(8,128)} fusion(bf16[512,2048]{1,0:T(8,128)(2,1)} %all-gather.5.cloned.1.call-done, bf16[2048,1792]{1,0:T(8,128)(2,1)} %param.8), kind=kOutput, calls=%fused_computation.27 | convolution fusion | flops 3758096384 | bytes 13107200 | tf_op jit(solution)/shard_map/dot_general | solution.py:52
  76.8 0.0 copy-start.3
  76.8 0.0 reduce-scatter.6.cloned.1.call-update
  76.8 0.0 reduce-scatter.8.cloned.1.call-start
  76.9 1.6 copy-done.3
  78.5 8.9 %fusion.7 = f32[512,1792]{1,0:T(8,128)} fusion(bf16[512,2048]{1,0:T(8,128)(2,1)S(1)} %copy-done.3, bf16[2048,1792]{1,0:T(8,128)(2,1)} %param.7), kind=kOutput, calls=%fused_computation.28 | convolution fusion | flops 3758096384 | bytes 13107200 | tf_op jit(solution)/shard_map/dot_general | solution.py:51
  87.3 0.0 reduce-scatter.8.cloned.1.call-update
  87.4 0.2 all-gather.7.cloned.1.call-start
  87.6 19.0 %reduce-scatter.4.cloned.1.call-done = f32[256,1792]{1,0:T(8,128)} async-done(((f32[512,1792]{1,0:T(8,128)}), f32[256,1792]{1,0:T(8,128)}) %reduce-scatter.4.cloned.1.call-update) | async-done | bytes 1835024 | tf_op jit(solution)/shard_map/reduce_scatter | solution.py:60
  106.6 51.8 %reduce-scatter.6.cloned.1.call-done = f32[256,1792]{1,0:T(8,128)} async-done(((f32[512,1792]{1,0:T(8,128)}), f32[256,1792]{1,0:T(8,128)}) %reduce-scatter.6.cloned.1.call-update) | async-done | bytes 1835024 | tf_op jit(solution)/shard_map/reduce_scatter | solution.py:58
  158.4 51.7 %reduce-scatter.8.cloned.1.call-done = f32[256,1792]{1,0:T(8,128)} async-done(((f32[512,1792]{1,0:T(8,128)}), f32[256,1792]{1,0:T(8,128)}) %reduce-scatter.8.cloned.1.call-update) | async-done | bytes 1835024 | tf_op jit(solution)/shard_map/reduce_scatter | solution.py:57
  210.1 5.0 %multiply_convert_fusion = (bf16[256,1792]{1,0:T(8,128)(2,1)}, bf16[256,1792]{1,0:T(8,128)(2,1)}, bf16[256,1792]{1,0:T(8,128)(2,1)}) fusion(f32[256,1792]{1,0:T(8,128)} %reduce-scatter.6.cloned.1.call-done, f32[256,1792]{1,0:T(8,128)} %reduce-scatter.8.cloned.1.call-done, f32[256,1792]{1,0:T(8,128)} %reduce-scatter.4.cloned.1.call-done), kind=kLoop, calls=%fused_computation.6 | loop fusion | flops 6881280 | bytes 8257536 | tf_op jit(solution)/shard_map/convert_element_type | solution.py:38
  215.1 0.0 all-gather.7.cloned.1.call-update
  215.1 0.0 all-gather.9.cloned.1.call-start
  215.2 0.7 all-gather.9.cloned.1.call-update
  215.9 0.0 all-gather.11.cloned.1.call-start
  215.9 0.7 all-gather.11.cloned.1.call-update
  216.6 28.6 %all-gather.7.cloned.1.call-done = bf16[512,1792]{1,0:T(8,128)(2,1)} async-done(((bf16[256,1792]{1,0:T(8,128)(2,1)}), bf16[512,1792]{1,0:T(8,128)(2,1)}) %all-gather.7.cloned.1.call-update) | async-done | bytes 1835024 | tf_op jit(solution)/shard_map/all_gather | solution.py:64
  245.3 7.5 %fusion = bf16[2048,1792]{0,1:T(8,128)(2,1)} fusion(bf16[512,1792]{1,0:T(8,128)(2,1)} %all-gather.7.cloned.1.call-done, bf16[512,2048]{1,0:T(8,128)(2,1)S(1)} %copy-done.3), kind=kOutput, calls=%fused_computation.4 | convolution fusion | flops 3761766400 | bytes 11272192 | tf_op jit(solution)/shard_map/dot_general | solution.py:30
  252.8 10.0 %copy.8 = bf16[2048,1792]{1,0:T(8,128)(2,1)} copy(bf16[2048,1792]{0,1:T(8,128)(2,1)} %fusion) | data formatting | bytes 14680064
  262.8 14.7 %all-gather.9.cloned.1.call-done = bf16[512,1792]{1,0:T(8,128)(2,1)} async-done(((bf16[256,1792]{1,0:T(8,128)(2,1)}), bf16[512,1792]{1,0:T(8,128)(2,1)}) %all-gather.9.cloned.1.call-update) | async-done | bytes 1835024 | tf_op jit(solution)/shard_map/all_gather | solution.py:65
  277.5 7.6 %fusion.1 = bf16[2048,1792]{0,1:T(8,128)(2,1)} fusion(bf16[512,1792]{1,0:T(8,128)(2,1)} %all-gather.9.cloned.1.call-done, bf16[512,2048]{1,0:T(8,128)(2,1)S(1)} %copy-done.3), kind=kOutput, calls=%fused_computation.5 | convolution fusion | flops 3761766400 | bytes 11272192 | tf_op jit(solution)/shard_map/dot_general | solution.py:30
  285.1 0.0 copy-start
  285.1 10.2 %copy.9 = bf16[2048,1792]{1,0:T(8,128)(2,1)} copy(bf16[2048,1792]{0,1:T(8,128)(2,1)} %fusion.1) | data formatting | bytes 14680064
  295.2 13.9 %all-gather.11.cloned.1.call-done = bf16[512,1792]{1,0:T(8,128)(2,1)} async-done(((bf16[256,1792]{1,0:T(8,128)(2,1)}), bf16[512,1792]{1,0:T(8,128)(2,1)}) %all-gather.11.cloned.1.call-update) | async-done | bytes 1835024 | tf_op jit(solution)/shard_map/all_gather | solution.py:63
  309.2 0.0 copy-done
  309.2 7.6 %convolution_convert_fusion = bf16[1792,2048]{1,0:T(8,128)(2,1)} fusion(bf16[512,1792]{1,0:T(8,128)(2,1)} %all-gather.11.cloned.1.call-done, bf16[512,2048]{1,0:T(8,128)(2,1)S(1)} %bitcast.36), kind=kOutput, calls=%fused_computation.1 | convolution fusion | flops 3761766400 | bytes 11272192 | tf_op jit(solution)/shard_map/dot_general | solution.py:30
  (8 shorter events, 0.1 us)
Async XLA Ops:
  8.0 38.9 %copy-start.1 = (bf16[64,2048]{1,0:T(8,128)(2,1)S(1)}, bf16[64,2048]{1,0:T(8,128)(2,1)}, u32[]{:S(2)}) copy-start(bf16[64,2048]{1,0:T(8,128)(2,1)} %param.6) | copy-start | bytes 786436
  8.0 59.3 %all-gather.5.cloned.1.call-start = ((), (), s32[]{:S(2)}) async-start(), calls=%async_computation.4 | async-start | bytes 2359296 | tf_op jit(solution)/shard_map/all_gather | solution.py:48
  8.1 8.8 %collective-permute-start = (bf16[64,2048]{1,0:T(8,128)(2,1)}, bf16[64,2048]{1,0:T(8,128)(2,1)S(1)}, u32[]{:S(2)}, u32[]{:S(2)}) collective-permute-start(bf16[64,2048]{1,0:T(8,128)(2,1)} %param.6), channel_id=1, source_target_pairs={{0,2},{2,4},{4,6},{6,8},{8,10},{10,12},{12,14},{14,0},{1,3},{3,5},... | collective-permute-start | bytes 786440 | tf_op jit(solution)/shard_map/ppermute | solution.py:20
  16.9 9.5 %collective-permute-start.1 = (bf16[64,2048]{1,0:T(8,128)(2,1)S(1)}, bf16[64,2048]{1,0:T(8,128)(2,1)S(1)}, u32[]{:S(2)}, u32[]{:S(2)}) collective-permute-start(bf16[64,2048]{1,0:T(8,128)(2,1)S(1)} %collective-permute-done), channel_id=1, source_target_pairs={{0,2},{2,4},{4,6},{6,8},{8,10},{10,12},{12,14},{14,0},{1,3},{3,5},... | collective-permute-start | bytes 786440 | tf_op jit(solution)/shard_map/ppermute | solution.py:20
  16.9 9.5 %collective-permute-start.4 = (bf16[64,2048]{1,0:T(8,128)(2,1)}, bf16[64,2048]{1,0:T(8,128)(2,1)S(1)}, u32[]{:S(2)}, u32[]{:S(2)}) collective-permute-start(bf16[64,2048]{1,0:T(8,128)(2,1)} %param.6), channel_id=1, source_target_pairs={{2,0},{4,2},{6,4},{8,6},{10,8},{12,10},{14,12},{0,14},{3,1},{5,3},... | collective-permute-start | bytes 786440 | tf_op jit(solution)/shard_map/ppermute | solution.py:22
  26.3 9.9 %collective-permute-start.2 = (bf16[64,2048]{1,0:T(8,128)(2,1)S(1)}, bf16[64,2048]{1,0:T(8,128)(2,1)S(1)}, u32[]{:S(2)}, u32[]{:S(2)}) collective-permute-start(bf16[64,2048]{1,0:T(8,128)(2,1)S(1)} %collective-permute-done.1), channel_id=1, source_target_pairs={{0,2},{2,4},{4,6},{6,8},{8,10},{10,12},{12,14},{14,0},{1,3},{3,5},... | collective-permute-start | bytes 786440 | tf_op jit(solution)/shard_map/ppermute | solution.py:20
  26.4 10.0 %collective-permute-start.5 = (bf16[64,2048]{1,0:T(8,128)(2,1)S(1)}, bf16[64,2048]{1,0:T(8,128)(2,1)S(1)}, u32[]{:S(2)}, u32[]{:S(2)}) collective-permute-start(bf16[64,2048]{1,0:T(8,128)(2,1)S(1)} %collective-permute-done.4), channel_id=1, source_target_pairs={{2,0},{4,2},{6,4},{8,6},{10,8},{12,10},{14,12},{0,14},{3,1},{5,3},... | collective-permute-start | bytes 786440 | tf_op jit(solution)/shard_map/ppermute | solution.py:22
  36.2 3.7 %copy-start.2 = (bf16[64,2048]{1,0:T(8,128)(2,1)}, bf16[64,2048]{1,0:T(8,128)(2,1)S(1)}, u32[]{:S(2)}) copy-start(bf16[64,2048]{1,0:T(8,128)(2,1)S(1)} %collective-permute-done.2) | copy-start | bytes 786436
  36.2 8.6 %collective-permute-start.3 = (bf16[64,2048]{1,0:T(8,128)(2,1)S(1)}, bf16[64,2048]{1,0:T(8,128)(2,1)}, u32[]{:S(2)}, u32[]{:S(2)}) collective-permute-start(bf16[64,2048]{1,0:T(8,128)(2,1)S(1)} %collective-permute-done.2), channel_id=1, source_target_pairs={{0,2},{2,4},{4,6},{6,8},{8,10},{10,12},{12,14},{14,0},{1,3},{3,5},... | collective-permute-start | bytes 786440 | tf_op jit(solution)/shard_map/ppermute | solution.py:20
  36.2 70.3 %reduce-scatter.4.cloned.1.call-start = ((), (), s32[]{:S(2)}) async-start(), calls=%async_computation.3 | async-start | bytes 5505024 | tf_op jit(solution)/shard_map/reduce_scatter | solution.py:60
  36.3 10.6 %collective-permute-start.6 = (bf16[64,2048]{1,0:T(8,128)(2,1)S(1)}, bf16[64,2048]{1,0:T(8,128)(2,1)S(1)}, u32[]{:S(2)}, u32[]{:S(2)}) collective-permute-start(bf16[64,2048]{1,0:T(8,128)(2,1)S(1)} %collective-permute-done.5), channel_id=1, source_target_pairs={{2,0},{4,2},{6,4},{8,6},{10,8},{12,10},{14,12},{0,14},{3,1},{5,3},... | collective-permute-start | bytes 786440 | tf_op jit(solution)/shard_map/ppermute | solution.py:22
  58.7 99.7 %reduce-scatter.6.cloned.1.call-start = ((), (), s32[]{:S(2)}) async-start(), calls=%async_computation.5 | async-start | bytes 5505024 | tf_op jit(solution)/shard_map/reduce_scatter | solution.py:58
  76.8 1.7 copy-start.3
  76.8 133.3 %reduce-scatter.8.cloned.1.call-start = ((), (), s32[]{:S(2)}) async-start(), calls=%async_computation.6 | async-start | bytes 5505024 | tf_op jit(solution)/shard_map/reduce_scatter | solution.py:57
  87.4 157.9 %all-gather.7.cloned.1.call-start = ((), (), s32[]{:S(2)}) async-start(), calls=%async_computation.7 | async-start | bytes 2752512 | tf_op jit(solution)/shard_map/all_gather | solution.py:64
  215.1 62.4 %all-gather.9.cloned.1.call-start = ((), (), s32[]{:S(2)}) async-start(), calls=%async_computation.8 | async-start | bytes 2752512 | tf_op jit(solution)/shard_map/all_gather | solution.py:65
  215.9 93.3 %all-gather.11.cloned.1.call-start = ((), (), s32[]{:S(2)}) async-start(), calls=%async_computation.9 | async-start | bytes 2752512 | tf_op jit(solution)/shard_map/all_gather | solution.py:63
  285.1 24.1 %copy-start = (bf16[8,64,2048]{2,1,0:T(8,128)(2,1)S(1)}, bf16[8,64,2048]{2,1,0:T(8,128)(2,1)}, u32[]{:S(2)}) copy-start(bf16[8,64,2048]{2,1,0:T(8,128)(2,1)} %gather_fusion) | copy-start | bytes 6291460
Sparse Core Ops, SparseCore 0:
  36.4 30.8 all-gather.4
Sparse Core Ops, SparseCore 1:
  58.8 47.7 reduce-scatter.3
  109.3 49.0 reduce-scatter.5
  161.1 49.0 reduce-scatter.7
  215.2 30.0 all-gather.6
  247.5 30.0 all-gather.8
  279.1 30.0 all-gather.10
